TPU v7x, 32 devices: a whole 2x2x4 slice. The times are simulated.
32 devices in a mesh: group: 2 (over y), batch: 8 (over z, x), tensor: 2 (over core).
Axes of the slice: x: 2, y: 2, z: 4, core: 2. Of those that a mesh axis runs over, the one named last changes fastest.
Arguments:
- hidden: bfloat16 [2, 2048, 8192], P(None, ('group', 'batch'), 'tensor'), parts along dimension 1, may hold values from -6 to 6
- value_projection_weight: bfloat16 [8192, 128], P('tensor'), may hold values from -0.0625 to 0.0625
- adapter_down_weight: bfloat16 [16, 8192, 64], P(('group', 'batch'), 'tensor'), parts along dimension 0, may hold values from -0.0625 to 0.0625
- adapter_up_weight: bfloat16 [16, 64, 128], P(('group', 'batch')), parts along dimension 0, may hold values from -0.75 to 0.75
- key_value_cache: bfloat16 [2048, 8, 256], P(('group', 'batch'), 'tensor'), parts along dimension 0, may hold values from -250 to 250
- query: bfloat16 [2, 2048, 1024], P(None, ('group', 'batch')), parts along dimension 1, may hold values from -6 to 6
- fresh_token_keys: bfloat16 [2, 2048, 128], P(None, ('group', 'batch')), parts along dimension 1, may hold values from -6 to 6
- adapter_per_row: int32 [2048, 1], P(('group', 'batch')), parts along dimension 0, may hold values from 0 to 7; in each aligned block of 128 rows (0 to 127, 128 to 255, ...) at most 16 rows name the same one
- cache_length: int32 [2048], P(('group', 'batch')), parts along dimension 0, may hold values from 1 to 8
- adapter_storage_index: int32 [16], P('group'), parts along dimension 0, may hold values from 0 to 7, each once
Outputs:
- context: bfloat16 [2, 2048, 1024], P(None, ('group', 'batch')), parts along dimension 1
There are 2 independent parts, one for each index of `group`. A program takes and returns all parts, laid end to end along the dimension named above; an argument that names none is the same for every part. Nothing has to cross between parts.
Inputs may be any that keep to these rules, and one draw needn't show every extreme that they name: `adapter_per_row`: in each aligned block of 128 rows (the rows of one device) no adapter is named by more than 16 rows, a bound that some block reaches. `adapter_storage_index`: each storage position holds exactly one adapter.
All inputs are finite; a program needn't handle non-finite values.
Results may differ from a plain program's by a relative error of at most 0.012.
Values may be sent and summed in bfloat16 or wider, within the bound.
A program may use at most 64 MiB of HBM per device.

v0:
```python
import jax
import jax.numpy as jnp
from jax import lax
from jax.sharding import PartitionSpec as P

HEAD_SIZE = 128
HQ = 8


adapter_scale = 1.0


def merged_2(array, axis, combine):
    everything = jax.tree.map(
        lambda part, kind: lax.all_gather(part.astype(kind), axis),
        array,
        (jnp.bfloat16, jnp.bfloat16, jnp.bfloat16),
    )

    def take(k):
        return jax.tree.map(lambda part, own: part[k].astype(own.dtype), everything, array)

    return lax.fori_loop(
        1, lax.axis_size(axis), lambda k, so_far: combine(so_far, take(k)), take(0)
    )


def combine(first, second):
    peak = jnp.maximum(first[0], second[0])
    left = jnp.exp(first[0] - peak)
    right = jnp.exp(second[0] - peak)
    return (
        peak,
        first[1] * left + second[1] * right,
        first[2] * left[..., None] + second[2] * right[..., None],
    )


def body(
    hidden,
    value_projection_weight,
    adapter_down_weight,
    adapter_up_weight,
    key_value_cache,
    query,
    fresh_token_keys,
    adapter_per_row,
    cache_length,
    adapter_storage_index,
):
    high = lax.Precision.HIGHEST
    nsteps, rows, half = hidden.shape
    peers = lax.axis_size("batch")
    slots = max(2, rows // peers)
    adapter = adapter_per_row[:, 0]
    count = adapter_storage_index.shape[0]
    match = adapter[:, None] == jnp.arange(count, dtype=jnp.int32)[None, :]
    held = jnp.sum(jnp.where(match, adapter_storage_index[None, :], 0), axis=1)
    onehot = (held[:, None] == jnp.arange(peers, dtype=jnp.int32)[None, :]).astype(jnp.int32)
    before = jnp.cumsum(onehot, axis=0) - onehot
    place = jnp.sum(before * onehot, axis=1)
    target = held * slots + place
    outgoing = jnp.zeros((nsteps, peers * slots, half), jnp.bfloat16).at[:, target].set(hidden)
    outgoing = outgoing.reshape(nsteps, peers, slots, half)
    local_down_matrix = adapter_down_weight[0]
    partial_shrink = jnp.einsum(
        "snkd,dr->snkr",
        lax.all_to_all(outgoing, "batch", split_axis=1, concat_axis=1, tiled=True),
        local_down_matrix,
        preferred_element_type=jnp.float32,
    )
    returned = lax.all_to_all(
        partial_shrink.astype(jnp.bfloat16), "batch", split_axis=1, concat_axis=1, tiled=True
    ).astype(partial_shrink.dtype)
    width = returned.shape[-1]
    per_row = returned.reshape(nsteps, peers * slots, width)[:, target]
    base_part = jnp.einsum(
        "srd,dh->srh", hidden, value_projection_weight, preferred_element_type=jnp.float32
    )
    adapter_tables = lax.all_gather(adapter_up_weight, "batch", axis=0, tiled=True)
    up_rows = adapter_tables[held].astype(jnp.float32)
    summand = base_part + adapter_scale * jnp.einsum(
        "srk,rkh->srh", per_row, up_rows, precision=high
    )
    new_value = lax.psum(summand.astype(jnp.bfloat16), "tensor")
    heads = query.reshape(nsteps, rows, HQ, HEAD_SIZE)
    inverse = HEAD_SIZE ** (-0.5)
    local_len = key_value_cache.shape[1]
    offset = lax.axis_index("tensor") * local_len
    positions = offset + jnp.arange(local_len, dtype=jnp.int32)
    cache_ok = (positions[None, :] < cache_length[:, None])[None, :, None, :]
    keys = key_value_cache[:, :, :HEAD_SIZE]
    values = key_value_cache[:, :, HEAD_SIZE:]
    scores = jnp.einsum("srhd,rld->srhl", heads, keys, preferred_element_type=jnp.float32) * inverse
    masked = jnp.where(cache_ok, scores, -1e30)
    peak = jnp.max(masked, axis=-1)
    weights = jnp.where(cache_ok, jnp.exp(masked - peak[..., None]), 0.0)
    total = jnp.sum(weights, axis=-1)
    summed = jnp.einsum(
        "srhl,rld->srhd", weights.astype(jnp.bfloat16), values, preferred_element_type=jnp.float32
    )
    merged = merged_2((peak, total, summed), "tensor", combine)
    steps_index = jnp.arange(2, dtype=jnp.int32)
    new_ok = (steps_index[None, :] <= steps_index[:, None])[:, None, None, :]
    own_scores = (
        jnp.einsum("srhd,jrd->srhj", heads, fresh_token_keys, preferred_element_type=jnp.float32)
        * inverse
    )
    own_masked = jnp.where(new_ok, own_scores, -1e30)
    own_peak = jnp.max(own_masked, axis=-1)
    own_weights = jnp.where(new_ok, jnp.exp(own_masked - own_peak[..., None]), 0.0)
    own_total = jnp.sum(own_weights, axis=-1)
    own_summed = jnp.einsum(
        "srhj,jrd->srhd",
        own_weights.astype(jnp.bfloat16),
        new_value,
        preferred_element_type=jnp.float32,
    )
    final = combine(merged, (own_peak, own_total, own_summed))
    context = final[2] / final[1][..., None]
    return context.reshape(nsteps, rows, HQ * HEAD_SIZE).astype(jnp.bfloat16)


def solution(mesh):
    in_specs = (
        P(None, ("group", "batch"), "tensor"),
        P("tensor", None),
        P(("group", "batch"), "tensor", None),
        P(("group", "batch"), None, None),
        P(("group", "batch"), "tensor", None),
        P(None, ("group", "batch"), None),
        P(None, ("group", "batch"), None),
        P(("group", "batch"), None),
        P(("group", "batch")),
        P("group"),
    )
    out_specs = P(None, ("group", "batch"), None)
    return jax.shard_map(body, mesh=mesh, in_specs=in_specs, out_specs=out_specs, check_vma=False)
```

profile of v0, /device:TPU:1, one launch (start us, length us, event | category | flops | bytes accessed | tf_op | source)
XLA Modules:
  0.0 162.8 jit_solution(2736290570409841477)
XLA Ops:
  6.5 0.0 copy-start
  6.5 0.9 select_reduce_fusion.1
  7.5 0.1 fusion.36
  7.6 0.2 reduce_window_sum.11
  7.7 0.2 select_reduce_fusion
  7.9 5.1 %copy.69 = bf16[128,2,4096]{2,1,0:T(2,128)(2,1)} copy(bf16[128,2,4096]{2,0,1:T(8,128)(2,1)} %bitcast.91) | data formatting | bytes 4194304 | tf_op args[0]
  13.1 2.1 %broadcast_in_dim.85 = bf16[2,128,4096]{2,0,1:T(2,128)(2,1)S(1)} broadcast(bf16[]{:T(256)} %constant.19.clone.1), dimensions={} | broadcast | bytes 2097154 | tf_op jit(solution)/shard_map/broadcast_in_dim | solution.py:63
  15.2 12.0 %scatter_fusion = bf16[2,128,4096]{2,0,1:T(2,128)(2,1)S(1)} fusion(bf16[2,128,4096]{2,0,1:T(2,128)(2,1)S(1)} %broadcast_in_dim.85, s32[128]{0:T(128)S(1)} %get-tuple-element.32, bf16[128,2,4096]{2,1,0:T(2,128)(2,1)} %copy.69), kind=kCustom, calls=%fused_computation.2 | custom fusion | bytes 6291968 | tf_op jit(solution)/shard_map/scatter | solution.py:63
  27.2 2.7 %copy.70 = bf16[2,8,16,4096]{3,2,0,1:T(8,128)(2,1)} copy(bf16[2,8,16,4096]{3,0,2,1:T(2,128)(2,1)S(1)} %bitcast.90) | data formatting | bytes 4194304 | tf_op jit(solution)/shard_map/reshape | solution.py:64
  29.8 0.0 copy-start.6
  29.8 6.5 %all-to-all-start = ((bf16[2,8,16,4096]{3,2,0,1:T(8,128)(2,1)}), bf16[2,8,16,4096]{3,2,0,1:T(8,128)(2,1)S(1)}, u32[]{:S(2)}, u32[]{:S(2)}) async-start(bf16[2,8,16,4096]{3,2,0,1:T(8,128)(2,1)} %copy.70), calls=%async_computation | async-start | bytes 4194304 | tf_op jit(solution)/shard_map/all_to_all | solution.py:68
  36.3 0.0 all-gather.5.cloned.1.call-start
  36.4 1.9 %copy.91 = bf16[32,8,8,128]{3,2,1,0:T(8,128)(2,1)} copy(bf16[32,8,8,128]{3,1,2,0:T(8,128)(2,1)} %bitcast.92) | data formatting | bytes 1048576
  38.3 0.0 copy-done.6
  38.3 0.1 broadcast_compare_fusion
  38.4 3.6 %fusion.51 = (f32[2,128,8]{2,0,1:T(2,128)S(1)}, f32[2,128,8,4]{2,3,0,1:T(4,128)S(1)}) fusion(bf16[128,4,256]{2,1,0:T(4,128)(2,1)} %param.14, pred[128,4]{1,0:T(8,128)(4,1)S(1)} %broadcast_compare_fusion, bf16[2,128,8,128]{3,2,1,0:T(8,128)(2,1)} %bitcast.93), kind=kOutput, calls=%fused_computation.78 | convolution fusion | flops 2119680 | bytes 696832 | tf_op jit(solution)/shard_map/srhd,rld->srhl/dot_general | solution.py:94
  42.0 0.0 copy-start.2
  42.0 0.0 copy-start.7
  42.0 0.8 copy-done.2
  42.8 2.3 %fusion.6 = bf16[2,128,8,128]{3,2,0,1:T(8,128)(2,1)} fusion(f32[2,128,8,4]{2,3,0,1:T(4,128)S(1)} %get-tuple-element.37, f32[2,128,8]{2,0,1:T(2,128)S(1)} %get-tuple-element.36, pred[128,4]{1,0:T(8,128)(4,1)S(1)} %broadcast_compare_fusion, bf16[128,4,256]{2,1,0:T(4,128)(2,1)} %param.14), kind=kOutput, calls=%fused_computation.11 | convolution fusion | flops 2383872 | bytes 696832 | tf_op jit(solution)/shard_map/srhl,rld->srhd/dot_general | solution.py:99
  45.1 0.0 all-gather.5.cloned.1.call-update
  45.2 0.1 copy.62
  45.2 1.7 %fusion.21 = bf16[2,128,8]{2,0,1:T(2,128)(2,1)S(1)} fusion(f32[2,128,8,4]{2,3,0,1:T(4,128)} %copy-done.2, f32[2,128,8]{2,0,1:T(2,128)S(1)} %get-tuple-element.36, pred[128,4]{1,0:T(8,128)(4,1)S(1)} %broadcast_compare_fusion), kind=kLoop, calls=%fused_computation.30 | loop fusion | flops 22528 | bytes 45568 | tf_op jit(solution)/shard_map/reduce_sum | solution.py:98
  46.9 0.1 copy.78
  47.0 0.0 copy-start.5
  47.0 0.0 copy-done.7
  47.0 4.2 %fusion.52 = (f32[2,128,8]{2,0,1:T(2,128)S(1)}, f32[2,128,8,2]{2,3,0,1:T(2,128)}) fusion(bf16[2,128,128,1]{2,1,0,3:T(8,128)(2,1)S(1)} %bitcast.98, pred[2,2]{1,0:T(4,128)(4,1)S(1)} %iota_compare_fusion.2, bf16[2,128,8,128]{3,2,1,0:T(8,128)(2,1)} %bitcast.94), kind=kOutput, calls=%fused_computation.79 | convolution fusion | flops 1058816 | bytes 614404 | tf_op jit(solution)/shard_map/srhd,jrd->srhj/dot_general | solution.py:106
  51.2 0.1 copy.67
  51.3 1.5 fusion.37
  52.9 0.0 copy-start.4
  52.9 0.1 copy.79
  52.9 0.0 copy-done.5
  52.9 30.7 %all-to-all-done = bf16[2,8,16,4096]{3,2,0,1:T(8,128)(2,1)S(1)} async-done(((bf16[2,8,16,4096]{3,2,0,1:T(8,128)(2,1)}), bf16[2,8,16,4096]{3,2,0,1:T(8,128)(2,1)S(1)}, u32[]{:S(2)}, u32[]{:S(2)}) %all-to-all-start) | async-done | bytes 2097184 | tf_op jit(solution)/shard_map/all_to_all | solution.py:68
  83.7 1.7 %fusion.12 = bf16[2,8,16,64]{3,2,1,0:T(8,128)(2,1)S(1)} fusion(bf16[2,8,16,4096]{3,2,0,1:T(8,128)(2,1)S(1)} %all-to-all-done, bf16[1,4096,64]{1,2,0:T(8,128)(2,1)} %param.12), kind=kOutput, calls=%fused_computation.20 | convolution fusion | flops 134234112 | bytes 2654208 | tf_op jit(solution)/shard_map/snkd,dr->snkr/dot_general | solution.py:66
  85.4 0.7 reshape.248
  86.2 4.7 %all-to-all-start.1 = ((bf16[8,2,1024]{2,1,0:T(2,128)(2,1)}), bf16[8,2,1024]{2,1,0:T(2,128)(2,1)S(1)}, u32[]{:S(2)}, u32[]{:S(2)}) async-start(bf16[8,2,1024]{2,1,0:T(2,128)(2,1)} %reshape.248), calls=%async_computation.1 | async-start | bytes 65536 | tf_op jit(solution)/shard_map/all_to_all | solution.py:72
  90.9 0.0 all-reduce.2.cloned.1.call-start
  90.9 0.0 copy-done.4
  90.9 24.6 %all_gather.20 = bf16[8,64,128]{2,1,0:T(8,128)(2,1)S(1)} all-gather(bf16[1,64,128]{2,1,0:T(8,128)(2,1)S(1)} %copy-done.4), channel_id=1, replica_groups=mesh['group'=2,'batch'=8,'tensor'=2] {'batch'}, dimensions={0}, use_global_device_ids=true | all-gather | bytes 147456 | tf_op jit(solution)/shard_map/all_gather | solution.py:80
  115.5 2.2 %gather_fusion = bf16[128,64,128]{2,1,0:T(8,128)(2,1)} fusion(bf16[8,64,128]{2,1,0:T(8,128)(2,1)S(1)} %all_gather.20, s32[1024]{0:T(1024)S(1)} %get-tuple-element.41), kind=kCustom, calls=%fused_computation | custom fusion | bytes 4194816 | tf_op jit(solution)/shard_map/gather | solution.py:81
  117.6 9.2 %all-gather.2 = bf16[4,128,8]{1,2,0:T(8,128)(2,1)} all-gather(bf16[2,128,8]{1,2,0:T(8,128)(2,1)S(1)} %copy.78), channel_id=4, replica_groups=mesh['group'=2,'batch'=8,'tensor'=2] {'tensor'}, dimensions={0}, use_global_device_ids=true | all-gather | bytes 12288 | tf_op jit(solution)/shard_map/all_gather | solution.py:15
  126.8 1.9 %all-gather.1 = bf16[4,128,8]{1,2,0:T(8,128)(2,1)} all-gather(bf16[2,128,8]{1,2,0:T(8,128)(2,1)S(1)} %copy.62), channel_id=3, replica_groups=mesh['group'=2,'batch'=8,'tensor'=2] {'tensor'}, dimensions={0}, use_global_device_ids=true | all-gather | bytes 12288 | tf_op jit(solution)/shard_map/all_gather | solution.py:15
  128.7 0.0 all-to-all-done.1
  128.7 0.1 reshape.249
  128.8 0.1 copy.73
  128.9 0.7 gather_fusion.1
  129.6 2.2 %fusion.33 = f32[128,128,2]{1,2,0:T(2,128)S(1)} fusion(bf16[128,64,128]{2,1,0:T(8,128)(2,1)} %gather_fusion, bf16[128,2,64]{2,1,0:T(2,128)(2,1)S(1)} %gather_fusion.1), kind=kOutput, calls=%fused_computation.42 | convolution fusion | flops 4194304 | bytes 2260992 | tf_op jit(solution)/shard_map/srk,rkh->srh/dot_general | solution.py:82
  131.9 0.0 copy-done
  131.9 0.0 copy-done.1
  131.9 0.0 copy-start.3
  131.9 1.3 fusion.11
  133.2 0.0 all-reduce.2.cloned.1.call-update
  133.2 0.7 fusion.44
  134.0 0.1 copy.63
  134.1 0.1 copy.64
  134.3 0.1 copy.68
  134.4 0.1 copy.77
  134.6 0.1 copy.80
  134.7 0.0 all-gather.5.cloned.1.call-done
  134.7 17.3 %all-reduce.2.cloned.1.call-done = bf16[2,128,128]{2,1,0:T(8,128)(2,1)} async-done(((bf16[2,128,128]{2,1,0:T(8,128)(2,1)}), bf16[2,128,128]{2,1,0:T(8,128)(2,1)}) %all-reduce.2.cloned.1.call-update) | async-done | bytes 65552 | tf_op jit(solution)/shard_map/psum | solution.py:85
  152.0 0.0 copy-done.3
  152.0 2.9 %fusion.5 = bf16[2,128,8,128]{3,2,0,1:T(8,128)(2,1)S(1)} fusion(bf16[4,128,8,128]{3,2,0,1:T(8,128)(2,1)} %all-gather.5.cloned.1.call-done, f32[2,128,8]{2,0,1:T(2,128)S(1)} %copy.80, f32[2,128,8]{2,0,1:T(2,128)S(1)} %copy.77, f32[2,128,8]{2,0,1:T(2,128)S(1)} %copy.68, f32[2,128,8]{2,0,1:T(2,128)S(1)} %copy.64, f32[2,128,8]{2,0,1:T(2,128)S(1)} %copy.63, ...), kind=kOutput, calls=%fused_computation.9 | convolution fusion | flops 3682304 | bytes 1703940 | tf_op jit(solution)/shard_map/srhj,jrd->srhd/dot_general | solution.py:113
  154.9 0.1 convert_element_type.158
  155.1 0.9 copy.81
  (6 shorter events, 0.0 us)
Async XLA Ops:
  6.5 125.3 %copy-start = (bf16[4096,128]{1,0:T(8,128)(2,1)S(1)}, bf16[4096,128]{1,0:T(8,128)(2,1)}, u32[]{:S(2)}) copy-start(bf16[4096,128]{1,0:T(8,128)(2,1)} %param.11) | copy-start | bytes 3145732
  29.8 8.5 %copy-start.6 = (s32[128]{0:T(128)S(1)}, s32[128]{0:T(128)}, u32[]{:S(2)}) copy-start(s32[128]{0:T(128)} %param.18) | copy-start | bytes 1540
  29.8 53.9 %all-to-all-start = ((bf16[2,8,16,4096]{3,2,0,1:T(8,128)(2,1)}), bf16[2,8,16,4096]{3,2,0,1:T(8,128)(2,1)S(1)}, u32[]{:S(2)}, u32[]{:S(2)}) async-start(bf16[2,8,16,4096]{3,2,0,1:T(8,128)(2,1)} %copy.70), calls=%async_computation | async-start | bytes 4194304 | tf_op jit(solution)/shard_map/all_to_all | solution.py:68
  36.3 98.4 %all-gather.5.cloned.1.call-start = ((), (), s32[]{:S(2)}) async-start(), calls=%async_computation.3 | async-start | bytes 1572864 | tf_op jit(solution)/shard_map/all_gather | solution.py:15
  42.0 0.8 copy-start.2
  42.0 5.0 %copy-start.7 = (bf16[2,128,128]{2,1,0:T(8,128)(2,1)S(1)}, bf16[2,128,128]{2,1,0:T(8,128)(2,1)}, u32[]{:S(2)}) copy-start(bf16[2,128,128]{2,1,0:T(8,128)(2,1)} %param.16) | copy-start | bytes 196612
  47.0 5.9 %copy-start.5 = (pred[2,2]{1,0:T(4,128)(4,1)}, pred[2,2]{1,0:T(4,128)(4,1)S(1)}, u32[]{:S(2)}) copy-start(pred[2,2]{1,0:T(4,128)(4,1)S(1)} %iota_compare_fusion.2) | copy-start | bytes 16
  52.9 38.0 %copy-start.4 = (bf16[1,64,128]{2,1,0:T(8,128)(2,1)S(1)}, bf16[1,64,128]{2,1,0:T(8,128)(2,1)}, u32[]{:S(2)}) copy-start(bf16[1,64,128]{2,1,0:T(8,128)(2,1)} %param.13) | copy-start | bytes 49156
  86.2 42.6 %all-to-all-start.1 = ((bf16[8,2,1024]{2,1,0:T(2,128)(2,1)}), bf16[8,2,1024]{2,1,0:T(2,128)(2,1)S(1)}, u32[]{:S(2)}, u32[]{:S(2)}) async-start(bf16[8,2,1024]{2,1,0:T(2,128)(2,1)} %reshape.248), calls=%async_computation.1 | async-start | bytes 65536 | tf_op jit(solution)/shard_map/all_to_all | solution.py:72
  90.9 61.1 %all-reduce.2.cloned.1.call-start = ((), (), s32[]{:S(2)}) async-start(), calls=%async_computation.2 | async-start | bytes 131072 | tf_op jit(solution)/shard_map/psum | solution.py:85
  117.6 14.2 %copy-start.1 = (bf16[2,128,4096]{2,1,0:T(8,128)(2,1)S(1)}, bf16[2,128,4096]{2,1,0:T(8,128)(2,1)}, u32[]{:S(2)}) copy-start(bf16[2,128,4096]{2,1,0:T(8,128)(2,1)} %param.10) | copy-start | bytes 6291460
  131.9 20.1 %copy-start.3 = (f32[2,128,8,2]{2,3,0,1:T(2,128)S(1)}, f32[2,128,8,2]{2,3,0,1:T(2,128)}, u32[]{:S(2)}) copy-start(f32[2,128,8,2]{2,3,0,1:T(2,128)} %get-tuple-element.39) | copy-start | bytes 49156
Sparse Core Ops, SparseCore 0:
  45.3 11.0 all-gather.4
  133.4 18.5 all-reduce.1
where the time goes:
time: 164 us; the launch traced here: 163 us
  waiting for transfers between devices  48.1 us (29%)
  blocking collectives  35.6 us (22%)
  local copies, waits for them, and re-layouts  30.5 us (19%)
  matrix products  18.4 us (11%)
  between operations  13.7 us (8%)
  starting transfers between devices  11.2 us (7%)
  other arithmetic  5.38 us (3%)
    all_to_all x1, waiting for transfers between devices, body(): lax.all_to_all(outgoing, 'batch', split_axis=1, concat_axis=1, tiled=True)  30.7 us
    all_gather x1, blocking collectives, body(): lax.all_gather(adapter_up_weight, 'batch', axis=0, tiled=True)  24.6 us
    psum x1, waiting for transfers between devices, body(): new_value = lax.psum(summand.astype(jnp.bfloat16), 'tensor')  17.3 us
    scatter x1, local copies, waits for them, and re-layouts, body(): jnp.zeros((nsteps, peers * slots, half), jnp.bfloat16).at[:, target]  12 us
    all_gather x2, blocking collectives, merged_2(): lax.all_gather(part.astype(kind), axis)  11.1 us
    unnamed x20, local copies, waits for them, and re-layouts  8.75 us
    all_to_all x1, starting transfers between devices, body(): lax.all_to_all(outgoing, 'batch', split_axis=1, concat_axis=1, tiled=True)  6.49 us
    all_to_all x1, starting transfers between devices, body(): lax.all_to_all(partial_shrink.astype(jnp.bfloat16), 'batch', split_axis=1...  4.68 us
  transfers between devices with their start and end apart: 4, of which 2 were waited for; matrix products, arithmetic and copies ran while one was open for 16% of the time, Pallas kernels for 0%

commit v1 on v0

--- a/solution.py
+++ b/solution.py
@@ -1,6 +1,8 @@
 import jax
 import jax.numpy as jnp
 from jax import lax
+from jax.experimental import pallas as pl
+from jax.experimental.pallas import tpu as pltpu
 from jax.sharding import PartitionSpec as P
 
 HEAD_SIZE = 128
@@ -121,6 +123,411 @@
     return context.reshape(nsteps, rows, HQ * HEAD_SIZE).astype(jnp.bfloat16)
 
 
+SLOTS = 16
+CHUNKS = 4
+NT = (((1,), (1,)), ((), ()))
+NN = (((1,), (0,)), ((), ()))
+
+
+def mm(a, b, dims=NN):
+    return lax.dot_general(a, b, dims, preferred_element_type=jnp.float32)
+
+
+def halves(value):
+    high = value.astype(jnp.bfloat16)
+    low = (value - high.astype(jnp.float32)).astype(jnp.bfloat16)
+    return high, low
+
+
+def fused_kernel(
+    hid, wv, down, up, cache, query, fresh, adapter, length, storage, out,
+    hb, wvb, ab, ub, qb, kb, fb, grouped, from_x, from_end,
+    deltas, to_x, to_end, base, vsend, vrecv, ctx, wnew, inv, lencol, unsort, nv,
+    lsem, asend, arecv, csem, gsend, grecv, rrecv, dsend, drecv, vsem,
+):
+    group = lax.axis_index("group")
+    me = lax.axis_index("batch")
+    t = lax.axis_index("tensor")
+    z, x = me // 2, me % 2
+    pz = z + 1 - 2 * (z % 2)
+    mid = ((z + 1) // 2) % 2
+    is_mid = mid == 1
+    is_end = mid == 0
+
+    def dev(zz, xx):
+        return (group, zz * 2 + xx, t)
+
+    peer = (group, me, 1 - t)
+    across = dev(z, 1 - x)
+    beside = dev(pz, x)
+    diagonal = dev(pz, 1 - x)
+    far = dev(3 - z, x)
+    onward = dev(pz + mid * (3 - z - pz), x)
+
+    def remote(src, dst, send, recv, to):
+        return pltpu.make_async_remote_copy(
+            src_ref=src, dst_ref=dst, send_sem=send, recv_sem=recv,
+            device_id=to, device_id_type=pl.DeviceIdType.MESH,
+        )
+
+    width = hb.shape[2]
+    step = width // CHUNKS
+    half_len = cache.shape[0]
+
+    local = [
+        pltpu.make_async_copy(hid, hb, lsem.at[0]),
+        pltpu.make_async_copy(wv, wvb, lsem.at[1]),
+        pltpu.make_async_copy(query, qb, lsem.at[2]),
+        pltpu.make_async_copy(fresh, fb, lsem.at[3]),
+        pltpu.make_async_copy(cache, kb.at[t], lsem.at[4]),
+        pltpu.make_async_copy(down, ab.at[0], lsem.at[5]),
+        pltpu.make_async_copy(up, ub.at[0], lsem.at[6]),
+    ]
+    for copy in local:
+        copy.start()
+
+    barrier = pltpu.get_barrier_semaphore()
+    for to in (peer, across, beside, diagonal):
+        pl.semaphore_signal(barrier, inc=1, device_id=to, device_id_type=pl.DeviceIdType.MESH)
+
+    @pl.when(is_mid)
+    def _():
+        pl.semaphore_signal(barrier, inc=1, device_id=far, device_id_type=pl.DeviceIdType.MESH)
+
+    pl.semaphore_wait(barrier, 4 + mid)
+
+    def piece(slot, k):
+        if k == 0:
+            return ub.at[slot]
+        return ab.at[slot, :, pl.ds((k - 1) * step, step)]
+
+    def own_piece(k):
+        return up if k == 0 else down.at[:, pl.ds((k - 1) * step, step)]
+
+    pieces = range(CHUNKS + 1)
+    own_out = [
+        remote(own_piece(k), piece(1 + mid, k), asend.at[0, k], arecv.at[1 + mid, k], onward)
+        for k in pieces
+    ]
+    for copy in own_out:
+        copy.start()
+    cache_out = remote(cache, kb.at[t], csem.at[0], csem.at[1], peer)
+    cache_out.start()
+
+    def forward(slot, k):
+        to, there = {1: (far, 3), 2: (beside, 2), 3: (beside, 3)}[slot]
+        return remote(piece(slot, k), piece(there, k), asend.at[slot, k], arecv.at[there, k], to)
+
+    def arrived(slot, k):
+        remote(piece(slot, k), piece(slot, k), asend.at[slot, k], arecv.at[slot, k], peer).wait_recv()
+
+    def relay(k, slots):
+        @pl.when(is_mid)
+        def _():
+            for slot in slots:
+                arrived(slot, k)
+                forward(slot, k).start()
+
+    names = adapter[...]
+    held = jnp.zeros_like(names)
+    for a in range(storage.shape[0]):
+        held = held + jnp.where(names == a, storage[a], 0)
+    rows = names.shape[1]
+    sub = lax.broadcasted_iota(jnp.int32, (rows, rows), 0)
+    lane = lax.broadcasted_iota(jnp.int32, (rows, rows), 1)
+    mine = lax.broadcasted_iota(jnp.int32, (8, rows), 0) == held
+    earlier = mm(mine.astype(jnp.bfloat16), (sub < lane).astype(jnp.bfloat16))
+    place = jnp.sum(jnp.where(mine, earlier, 0.0), axis=0, keepdims=True).astype(jnp.int32)
+    hz = lax.shift_right_logical(held, 1)
+    xrel = (held + x) & 1
+    outer = jnp.where((hz == 1) | (hz == 2), 2, 3)
+    same_side = lax.shift_right_logical(hz, 1) == z // 2
+    relation = jnp.where(hz == z, 0, jnp.where(same_side, 1, outer))
+    target = (relation * 2 + xrel) * SLOTS + place
+    sort = (sub == target).astype(jnp.bfloat16)
+    diag = sub == lane
+    column = jnp.sum(jnp.where(diag, target, 0), axis=1, keepdims=True)
+    unsort[...] = (column == lane).astype(jnp.bfloat16)
+    lencol[...] = jnp.sum(jnp.where(diag, length[...], 0), axis=1, keepdims=True)
+
+    local[0].wait()
+    for k in range(CHUNKS):
+        cols = pl.ds(k * step, step)
+        for s in range(2):
+            moved = mm(sort, hb[s, :, cols]).astype(jnp.bfloat16)
+            for g in range(8):
+                grouped[g, s * SLOTS:(s + 1) * SLOTS, cols] = moved[g * SLOTS:(g + 1) * SLOTS]
+
+    def rows_across(q):
+        return remote(grouped.at[2 * q + 1], from_x.at[q], gsend.at[2 * q + 1], grecv.at[q], across)
+
+    rows_beside = remote(grouped.at[2], from_end.at[0], gsend.at[2], rrecv.at[0], beside)
+    rows_diagonal = remote(grouped.at[3], from_end.at[1], gsend.at[3], rrecv.at[1], diagonal)
+    rows_across(0).start()
+    rows_across(2).start()
+
+    @pl.when(is_mid)
+    def _():
+        rows_across(1).start()
+
+    @pl.when(is_end)
+    def _():
+        rows_beside.start()
+        rows_diagonal.start()
+
+    rows_across(3).start()
+    relay(0, (2, 1))
+
+    local[1].wait()
+    for s in range(2):
+        base[s] = mm(hb[s], wvb[...])
+    relay(1, (2, 1))
+
+    for copy in local[2:]:
+        copy.wait()
+    cache_out.wait_recv()
+    positions = half_len // rows
+    cached = 2 * positions * SLOTS
+    inverse = HEAD_SIZE ** (-0.5)
+
+    def attend(b, carry):
+        at = pl.ds(pl.multiple_of(b * SLOTS, SLOTS), SLOTS)
+        cat = pl.ds(pl.multiple_of(b * SLOTS * positions, SLOTS * positions), SLOTS * positions)
+        q = jnp.concatenate(
+            [qb[s, at, h * HEAD_SIZE:(h + 1) * HEAD_SIZE] for s in range(2) for h in range(HQ)], axis=0
+        )
+        keys = jnp.concatenate(
+            [kb[0, cat, :HEAD_SIZE], kb[1, cat, :HEAD_SIZE], fb[0, at, :], fb[1, at, :]], axis=0
+        )
+        scores = mm(q, keys, NT) * inverse
+        i = lax.broadcasted_iota(jnp.int32, scores.shape, 0)
+        c = lax.broadcasted_iota(jnp.int32, scores.shape, 1)
+        per_half = SLOTS * positions
+        in_cache = c < cached
+        row_of = jnp.where(in_cache, (c % per_half) // positions, c % SLOTS)
+        position = (c // per_half) * positions + c % positions
+        limits = jnp.concatenate([lencol[at, :]] * (2 * HQ), axis=0)
+        order = jnp.where(in_cache, position, (c - cached) // SLOTS)
+        bound = jnp.where(in_cache, limits, i // (SLOTS * HQ) + 1)
+        ok = (order < bound) & (row_of == i % SLOTS)
+        masked = jnp.where(ok, scores, -1e30)
+        peak = jnp.max(masked, axis=1, keepdims=True)
+        weights = jnp.where(ok, jnp.exp(masked - peak), 0.0)
+        inv[b] = 1.0 / jnp.sum(weights, axis=1, keepdims=True)
+        rounded = weights.astype(jnp.bfloat16)
+        values = jnp.concatenate([kb[0, cat, HEAD_SIZE:], kb[1, cat, HEAD_SIZE:]], axis=0)
+        ctx[b] = mm(rounded[:, :cached], values)
+        wnew[b] = rounded[:, cached:]
+        return carry
+
+    blocks = rows // SLOTS
+    lax.fori_loop(0, 3, attend, 0)
+    relay(2, (2, 1))
+    lax.fori_loop(3, 6, attend, 0)
+    relay(3, (2, 1))
+    lax.fori_loop(6, blocks, attend, 0)
+    relay(4, (2, 1))
+
+    def project(first, second, slot, cols, so_far):
+        both = jnp.concatenate([first[:, cols], second[:, cols]], axis=0)
+        part = mm(both, ab[slot, :, cols], NT)
+        return part if so_far is None else so_far + part
+
+    def expand(shrink, slot):
+        high, low = halves(shrink)
+        return mm(high, ub[slot]) + mm(low, ub[slot])
+
+    def delta_out(q):
+        return remote(to_x.at[q], deltas.at[2 * q + 1], dsend.at[q], drecv.at[2 * q + 1], across)
+
+    def finish(q, slot, shrink):
+        delta = expand(shrink, slot)
+        deltas[2 * q] = delta[:2 * SLOTS]
+        to_x[q] = delta[2 * SLOTS:]
+        delta_out(q).start()
+
+    def relation_of(q, each=None):
+        rows_across(q).wait_recv()
+        shrink = None
+        for k in range(CHUNKS):
+            if each is not None:
+                each(k)
+            shrink = project(grouped.at[2 * q], from_x.at[q], q, pl.ds(k * step, step), shrink)
+        finish(q, q, shrink)
+
+    relation_of(0)
+
+    @pl.when(is_end)
+    def _():
+        for k in pieces:
+            arrived(2, k)
+
+    relation_of(2)
+
+    @pl.when(is_mid)
+    def _():
+        relation_of(1)
+        for k in pieces:
+            arrived(3, k)
+            forward(3, k).start()
+
+    result_beside = remote(to_end.at[0], deltas.at[2], dsend.at[4], drecv.at[2], beside)
+    result_diagonal = remote(to_end.at[1], deltas.at[3], dsend.at[5], drecv.at[3], diagonal)
+
+    @pl.when(is_mid)
+    def _():
+        rows_beside.wait_recv()
+        rows_diagonal.wait_recv()
+        shrink = None
+        for k in range(CHUNKS):
+            shrink = project(from_end.at[0], from_end.at[1], 0, pl.ds(k * step, step), shrink)
+        delta = expand(shrink, 0)
+        to_end[0] = delta[:2 * SLOTS]
+        to_end[1] = delta[2 * SLOTS:]
+        result_beside.start()
+        result_diagonal.start()
+        relation_of(3)
+
+    @pl.when(is_end)
+    def _():
+        arrived(3, 0)
+        relation_of(3, lambda k: arrived(3, k + 1))
+        result_beside.wait_recv()
+        result_diagonal.wait_recv()
+
+    @pl.when(is_mid)
+    def _():
+        delta_out(1).wait_recv()
+
+    for q in (0, 2, 3):
+        delta_out(q).wait_recv()
+
+    for s in range(2):
+        ordered = jnp.concatenate([deltas[g, s * SLOTS:(s + 1) * SLOTS, :] for g in range(8)], axis=0)
+        high, low = halves(ordered)
+        vsend[s] = base[s] + adapter_scale * (mm(unsort[...], high) + mm(unsort[...], low))
+    value_out = remote(vsend, vrecv, vsem.at[0], vsem.at[1], peer)
+    value_out.start()
+    value_out.wait_recv()
+    nv[...] = (vsend[...] + vrecv[...]).astype(jnp.bfloat16)
+
+    def close(b, carry):
+        at = pl.ds(pl.multiple_of(b * SLOTS, SLOTS), SLOTS)
+        fresh_values = jnp.concatenate([nv[0, at, :], nv[1, at, :]], axis=0)
+        result = ((ctx[b] + mm(wnew[b], fresh_values)) * inv[b]).astype(out.dtype)
+        for s in range(2):
+            for h in range(HQ):
+                first = (s * HQ + h) * SLOTS
+                out[s, at, h * HEAD_SIZE:(h + 1) * HEAD_SIZE] = result[first:first + SLOTS]
+        return carry
+
+    lax.fori_loop(0, blocks, close, 0)
+
+    value_out.wait_send()
+    cache_out.wait_send()
+    for copy in own_out:
+        copy.wait_send()
+    for q in (0, 2, 3):
+        rows_across(q).wait_send()
+        delta_out(q).wait_send()
+
+    @pl.when(is_end)
+    def _():
+        rows_beside.wait_send()
+        rows_diagonal.wait_send()
+
+    @pl.when(is_mid)
+    def _():
+        rows_across(1).wait_send()
+        delta_out(1).wait_send()
+        result_beside.wait_send()
+        result_diagonal.wait_send()
+        for slot in (1, 2, 3):
+            for k in pieces:
+                forward(slot, k).wait_send()
+
+
+def fused_body(
+    hidden,
+    value_projection_weight,
+    adapter_down_weight,
+    adapter_up_weight,
+    key_value_cache,
+    query,
+    fresh_token_keys,
+    adapter_per_row,
+    cache_length,
+    adapter_storage_index,
+):
+    bf16, f32 = jnp.bfloat16, jnp.float32
+    _, rows, width = hidden.shape
+    rank = adapter_down_weight.shape[2]
+    local_len = key_value_cache.shape[1]
+    down = jnp.swapaxes(adapter_down_weight[0], 0, 1)
+    cache = key_value_cache.reshape(rows * local_len, 2 * HEAD_SIZE)
+    blocks, tall = rows // SLOTS, 2 * HQ * SLOTS
+    anywhere = pl.BlockSpec(memory_space=pl.ANY)
+    vmem = pl.BlockSpec(memory_space=pltpu.VMEM)
+    dma = pltpu.SemaphoreType.DMA
+    return pl.pallas_call(
+        fused_kernel,
+        out_shape=jax.ShapeDtypeStruct(query.shape, bf16),
+        in_specs=[anywhere] * 7 + [vmem, vmem, pl.BlockSpec(memory_space=pltpu.SMEM)],
+        out_specs=vmem,
+        scratch_shapes=[
+            pltpu.VMEM(hidden.shape, bf16),
+            pltpu.VMEM((width, HEAD_SIZE), bf16),
+            pltpu.VMEM((4, rank, width), bf16),
+            pltpu.VMEM((4, rank, HEAD_SIZE), bf16),
+            pltpu.VMEM(query.shape, bf16),
+            pltpu.VMEM((2,) + cache.shape, bf16),
+            pltpu.VMEM(fresh_token_keys.shape, bf16),
+            pltpu.VMEM((8, 2 * SLOTS, width), bf16),
+            pltpu.VMEM((4, 2 * SLOTS, width), bf16),
+            pltpu.VMEM((2, 2 * SLOTS, width), bf16),
+            pltpu.VMEM((8, 2 * SLOTS, HEAD_SIZE), f32),
+            pltpu.VMEM((4, 2 * SLOTS, HEAD_SIZE), f32),
+            pltpu.VMEM((2, 2 * SLOTS, HEAD_SIZE), f32),
+            pltpu.VMEM((2, rows, HEAD_SIZE), f32),
+            pltpu.VMEM((2, rows, HEAD_SIZE), f32),
+            pltpu.VMEM((2, rows, HEAD_SIZE), f32),
+            pltpu.VMEM((blocks, tall, HEAD_SIZE), f32),
+            pltpu.VMEM((blocks, tall, 2 * SLOTS), bf16),
+            pltpu.VMEM((blocks, tall, 1), f32),
+            pltpu.VMEM((rows, 1), jnp.int32),
+            pltpu.VMEM((rows, rows), bf16),
+            pltpu.VMEM((2, rows, HEAD_SIZE), bf16),
+            dma((7,)),
+            dma((4, CHUNKS + 1)),
+            dma((4, CHUNKS + 1)),
+            dma((2,)),
+            dma((8,)),
+            dma((4,)),
+            dma((2,)),
+            dma((6,)),
+            dma((8,)),
+            dma((2,)),
+        ],
+        compiler_params=pltpu.CompilerParams(
+            collective_id=0, has_side_effects=True, vmem_limit_bytes=40 * 1024 * 1024
+        ),
+        cost_estimate=pl.CostEstimate(
+            flops=2 * 4 * rows * width * HEAD_SIZE, bytes_accessed=6 << 20, transcendentals=rows * 2560
+        ),
+    )(
+        hidden,
+        value_projection_weight,
+        down,
+        adapter_up_weight[0],
+        cache,
+        query,
+        fresh_token_keys,
+        adapter_per_row.reshape(1, rows),
+        cache_length.reshape(1, rows),
+        adapter_storage_index,
+    )
+
+
 def solution(mesh):
     in_specs = (
         P(None, ("group", "batch"), "tensor"),
@@ -135,4 +542,6 @@
         P("group"),
     )
     out_specs = P(None, ("group", "batch"), None)
-    return jax.shard_map(body, mesh=mesh, in_specs=in_specs, out_specs=out_specs, check_vma=False)
+    small = mesh.shape["batch"] == 8 and mesh.shape["tensor"] == 2
+    chosen = fused_body if small else body
+    return jax.shard_map(chosen, mesh=mesh, in_specs=in_specs, out_specs=out_specs, check_vma=False)

time: 164 us -> 56.3 us (0.34)
  waiting for transfers between devices: 48.1 us -> 0 us
  Pallas kernels: 0 us -> 45.6 us
  blocking collectives: 35.6 us -> 0 us
  local copies, waits for them, and re-layouts: 30.5 us -> 10.2 us
  matrix products: 18.4 us -> 0 us
  between operations: 13.7 us -> 0.03 us
  starting transfers between devices: 11.2 us -> 0 us
  other arithmetic: 5.38 us -> 0 us
    pallas_call x0 -> x1, Pallas kernels: none -> 45.6 us  [fused_body(): pl.pallas_call(fused_kernel, out_shape=jax.ShapeDtypeStruct(query.shape,...]
    all_gather x3 -> x0, blocking collectives: 35.6 us -> none  [the longest x1 24.6 us: body(): lax.all_gather(adapter_up_weight, 'batch', axis=0, tiled=True)]
    all_to_all x2 -> x0, waiting for transfers between devices: 30.7 us -> none  [the longest x1 30.7 us: body(): lax.all_to_all(outgoing, 'batch', split_axis=1, concat_axis=1, tiled=True)]
    dot_general x7 -> x0, matrix products: 18.4 us -> none  [the longest x1 4.23 us: body(): jnp.einsum('srhd,jrd->srhj', heads, fresh_token_keys, preferred_element_t...]
    psum x1 -> x0, waiting for transfers between devices: 17.3 us -> none  [body(): new_value = lax.psum(summand.astype(jnp.bfloat16), 'tensor')]
    scatter x1 -> x0, local copies, waits for them, and re-layouts: 12 us -> none  [body(): jnp.zeros((nsteps, peers * slots, half), jnp.bfloat16).at[:, target]]
    all_to_all x2 -> x0, starting transfers between devices: 11.2 us -> none  [the longest x1 6.49 us: body(): lax.all_to_all(outgoing, 'batch', split_axis=1, concat_axis=1, tiled=True)]
    reduce_sum x4 -> x0, other arithmetic: 4.3 us -> none  [the longest x1 1.66 us: body(): total = jnp.sum(weights, axis=-1)]
  transfers between devices with their start and end apart: 4 -> 0, of which waited for: 2 -> 0; matrix products, arithmetic and copies ran while one was open for 16% -> 0% of each run, Pallas kernels for 0% -> 0%
where the time goes in v1:
time: 56.3 us; the launch traced here: 55.8 us
  Pallas kernels  45.6 us (81%)
  local copies, waits for them, and re-layouts  10.2 us (18%)
    pallas_call x1, Pallas kernels, fused_body(): pl.pallas_call(fused_kernel, out_shape=jax.ShapeDtypeStruct(query.shape,...  45.6 us
    unnamed x19, local copies, waits for them, and re-layouts  9.21 us

profile of v1, /device:TPU:1, one launch (start us, length us, event | category | flops | bytes accessed | tf_op | source)
XLA Modules:
  0.0 55.8 jit_solution(8884774301638246557)
XLA Ops:
  0.0 1.0 %reshape.9.cache = bf16[512,256]{1,0:T(8,128)(2,1)S(1)} reshape(bf16[128,4,256]{2,1,0:T(4,128)(2,1)} %param.14) | data formatting | bytes 524288 | tf_op jit(solution)/shard_map/reshape | solution.py:467
  1.0 0.0 copy-start
  1.0 1.6 %copy-done = bf16[2,128,4096]{2,1,0:T(8,128)(2,1)S(1)} copy-done((bf16[2,128,4096]{2,1,0:T(8,128)(2,1)S(1)}, bf16[2,128,4096]{2,1,0:T(8,128)(2,1)}, u32[]{:S(2)}) %copy-start) | copy-done | bytes 2097176
  2.6 0.0 copy-start.1
  2.6 1.2 %copy-done.1 = bf16[4096,128]{1,0:T(8,128)(2,1)S(1)} copy-done((bf16[4096,128]{1,0:T(8,128)(2,1)S(1)}, bf16[4096,128]{1,0:T(8,128)(2,1)}, u32[]{:S(2)}) %copy-start.1) | copy-done | bytes 1048600
  3.8 0.0 copy-start.2
  3.8 1.0 %copy-done.2 = bf16[1,4096,64]{1,2,0:T(8,128)(2,1)S(1)} copy-done((bf16[1,4096,64]{1,2,0:T(8,128)(2,1)S(1)}, bf16[1,4096,64]{1,2,0:T(8,128)(2,1)}, u32[]{:S(2)}) %copy-start.2) | copy-done | bytes 524312
  4.9 0.0 copy-start.3
  4.9 1.0 %copy-done.3 = bf16[2,128,1024]{2,1,0:T(8,128)(2,1)S(1)} copy-done((bf16[2,128,1024]{2,1,0:T(8,128)(2,1)S(1)}, bf16[2,128,1024]{2,1,0:T(8,128)(2,1)}, u32[]{:S(2)}) %copy-start.3) | copy-done | bytes 524312
  5.9 0.0 copy-start.4
  5.9 0.8 %copy-done.4 = bf16[2,128,128]{2,1,0:T(8,128)(2,1)S(1)} copy-done((bf16[2,128,128]{2,1,0:T(8,128)(2,1)S(1)}, bf16[2,128,128]{2,1,0:T(8,128)(2,1)}, u32[]{:S(2)}) %copy-start.4) | copy-done | bytes 65560
  6.8 0.0 copy-start.5
  6.8 0.7 %copy-done.5 = bf16[1,64,128]{2,1,0:T(8,128)(2,1)S(1)} copy-done((bf16[1,64,128]{2,1,0:T(8,128)(2,1)S(1)}, bf16[1,64,128]{2,1,0:T(8,128)(2,1)}, u32[]{:S(2)}) %copy-start.5) | copy-done | bytes 16408
  7.5 0.0 copy-start.6
  7.5 0.7 %copy-done.6 = s32[128,1]{0,1:T(1,128)S(1)} copy-done((s32[128,1]{0,1:T(1,128)S(1)}, s32[128,1]{0,1:T(1,128)}, u32[]{:S(2)}) %copy-start.6) | copy-done | bytes 536
  8.1 0.0 copy-start.7
  8.1 0.7 %copy-done.7 = s32[128]{0:T(128)S(1)} copy-done((s32[128]{0:T(128)S(1)}, s32[128]{0:T(128)}, u32[]{:S(2)}) %copy-start.7) | copy-done | bytes 536
  8.8 0.0 copy-start.8
  8.8 0.7 %copy-done.8 = s32[8]{0:T(128)S(1)} copy-done((s32[8]{0:T(128)S(1)}, s32[8]{0:T(128)}, u32[]{:S(2)}) %copy-start.8) | copy-done | bytes 56
  9.4 45.6 %shard_map.100 = bf16[2,128,1024]{2,1,0:T(8,128)(2,1)S(1)} custom-call(bf16[2,128,4096]{2,1,0:T(8,128)(2,1)S(1)} %copy-done, bf16[4096,128]{1,0:T(8,128)(2,1)S(1)} %copy-done.1, bf16[64,4096]{1,0:T(8,128)(2,1)S(1)} %bitcast.6, bf16[64,128]{1,0:T(8,128)(2,1)S(1)} %bitcast.7, bf16[512,256]{1,0:T(8,128)(2,1)S(1)} %reshape.9.cache, ...), custom_call_target="tpu_custom_call" | custom-call | flops 536870912 | bytes 6291456 | tf_op jit(solution)/shard_map/pallas_call | solution.py:472
  55.0 0.8 %copy.12 = bf16[2,128,1024]{2,1,0:T(8,128)(2,1)} copy(bf16[2,128,1024]{2,1,0:T(8,128)(2,1)S(1)} %shard_map.100) | data formatting | bytes 1048576
Async XLA Ops:
  1.0 1.6 %copy-start = (bf16[2,128,4096]{2,1,0:T(8,128)(2,1)S(1)}, bf16[2,128,4096]{2,1,0:T(8,128)(2,1)}, u32[]{:S(2)}) copy-start(bf16[2,128,4096]{2,1,0:T(8,128)(2,1)} %hid.1) | copy-start | bytes 6291460
  2.6 1.2 %copy-start.1 = (bf16[4096,128]{1,0:T(8,128)(2,1)S(1)}, bf16[4096,128]{1,0:T(8,128)(2,1)}, u32[]{:S(2)}) copy-start(bf16[4096,128]{1,0:T(8,128)(2,1)} %wv.1) | copy-start | bytes 3145732
  3.8 1.0 %copy-start.2 = (bf16[1,4096,64]{1,2,0:T(8,128)(2,1)S(1)}, bf16[1,4096,64]{1,2,0:T(8,128)(2,1)}, u32[]{:S(2)}) copy-start(bf16[1,4096,64]{1,2,0:T(8,128)(2,1)} %param.12) | copy-start | bytes 1572868
  4.9 1.0 %copy-start.3 = (bf16[2,128,1024]{2,1,0:T(8,128)(2,1)S(1)}, bf16[2,128,1024]{2,1,0:T(8,128)(2,1)}, u32[]{:S(2)}) copy-start(bf16[2,128,1024]{2,1,0:T(8,128)(2,1)} %query.1) | copy-start | bytes 1572868
  5.9 0.8 %copy-start.4 = (bf16[2,128,128]{2,1,0:T(8,128)(2,1)S(1)}, bf16[2,128,128]{2,1,0:T(8,128)(2,1)}, u32[]{:S(2)}) copy-start(bf16[2,128,128]{2,1,0:T(8,128)(2,1)} %fresh.1) | copy-start | bytes 196612
  6.8 0.7 %copy-start.5 = (bf16[1,64,128]{2,1,0:T(8,128)(2,1)S(1)}, bf16[1,64,128]{2,1,0:T(8,128)(2,1)}, u32[]{:S(2)}) copy-start(bf16[1,64,128]{2,1,0:T(8,128)(2,1)} %param.13) | copy-start | bytes 49156
  7.5 0.7 %copy-start.6 = (s32[128,1]{0,1:T(1,128)S(1)}, s32[128,1]{0,1:T(1,128)}, u32[]{:S(2)}) copy-start(s32[128,1]{0,1:T(1,128)} %param.17) | copy-start | bytes 1540
  8.1 0.7 %copy-start.7 = (s32[128]{0:T(128)S(1)}, s32[128]{0:T(128)}, u32[]{:S(2)}) copy-start(s32[128]{0:T(128)} %param.18) | copy-start | bytes 1540
  8.8 0.7 %copy-start.8 = (s32[8]{0:T(128)S(1)}, s32[8]{0:T(128)}, u32[]{:S(2)}) copy-start(s32[8]{0:T(128)} %storage.1) | copy-start | bytes 100

commit v2 on v1

--- a/solution.py
+++ b/solution.py
@@ -140,7 +140,8 @@
 
 
 def fused_kernel(
-    hid, wv, down, up, cache, query, fresh, adapter, length, storage, out,
+    hid, wv, down, up, cache, query, fresh, adapter_in, length_in, storage_in, out,
+    adapter, length, storage,
     hb, wvb, ab, ub, qb, kb, fb, grouped, from_x, from_end,
     deltas, to_x, to_end, base, vsend, vrecv, ctx, wnew, inv, lencol, unsort, nv,
     lsem, asend, arecv, csem, gsend, grecv, rrecv, dsend, drecv, vsem,
@@ -175,6 +176,9 @@
     half_len = cache.shape[0]
 
     local = [
+        pltpu.make_async_copy(adapter_in, adapter, lsem.at[7]),
+        pltpu.make_async_copy(length_in, length, lsem.at[8]),
+        pltpu.make_async_copy(storage_in, storage, lsem.at[9]),
         pltpu.make_async_copy(hid, hb, lsem.at[0]),
         pltpu.make_async_copy(wv, wvb, lsem.at[1]),
         pltpu.make_async_copy(query, qb, lsem.at[2]),
@@ -197,20 +201,18 @@
     pl.semaphore_wait(barrier, 4 + mid)
 
     def piece(slot, k):
-        if k == 0:
+        if k == CHUNKS:
             return ub.at[slot]
-        return ab.at[slot, :, pl.ds((k - 1) * step, step)]
-
-    def own_piece(k):
-        return up if k == 0 else down.at[:, pl.ds((k - 1) * step, step)]
+        return ab.at[slot, :, pl.ds(k * step, step)]
+
+    def own_out(k):
+        src = up if k == CHUNKS else down.at[:, pl.ds(k * step, step)]
+        return remote(src, piece(1 + mid, k), asend.at[0, k], arecv.at[1 + mid, k], onward)
 
     pieces = range(CHUNKS + 1)
-    own_out = [
-        remote(own_piece(k), piece(1 + mid, k), asend.at[0, k], arecv.at[1 + mid, k], onward)
-        for k in pieces
-    ]
-    for copy in own_out:
-        copy.start()
+    own_out(CHUNKS).start()
+    own_out(0).start()
+    own_out(1).start()
     cache_out = remote(cache, kb.at[t], csem.at[0], csem.at[1], peer)
     cache_out.start()
 
@@ -221,13 +223,13 @@
     def arrived(slot, k):
         remote(piece(slot, k), piece(slot, k), asend.at[slot, k], arecv.at[slot, k], peer).wait_recv()
 
-    def relay(k, slots):
-        @pl.when(is_mid)
-        def _():
-            for slot in slots:
-                arrived(slot, k)
-                forward(slot, k).start()
-
+    def relay(slot, k):
+        for j in ((CHUNKS, 0) if k == 0 else (k,)):
+            arrived(slot, j)
+            forward(slot, j).start()
+
+    for copy in local[:3]:
+        copy.wait()
     names = adapter[...]
     held = jnp.zeros_like(names)
     for a in range(storage.shape[0]):
@@ -250,7 +252,7 @@
     unsort[...] = (column == lane).astype(jnp.bfloat16)
     lencol[...] = jnp.sum(jnp.where(diag, length[...], 0), axis=1, keepdims=True)
 
-    local[0].wait()
+    local[3].wait()
     for k in range(CHUNKS):
         cols = pl.ds(k * step, step)
         for s in range(2):
@@ -268,22 +270,29 @@
 
     @pl.when(is_mid)
     def _():
-        rows_across(1).start()
-
-    @pl.when(is_end)
-    def _():
-        rows_beside.start()
-        rows_diagonal.start()
-
-    rows_across(3).start()
-    relay(0, (2, 1))
-
-    local[1].wait()
+        relay(2, 0)
+        own_out(2).start()
+
+    @pl.when(is_end)
+    def _():
+        own_out(0).wait_send()
+        own_out(2).start()
+
+    local[4].wait()
     for s in range(2):
         base[s] = mm(hb[s], wvb[...])
-    relay(1, (2, 1))
-
-    for copy in local[2:]:
+
+    @pl.when(is_mid)
+    def _():
+        relay(2, 1)
+        own_out(3).start()
+
+    @pl.when(is_end)
+    def _():
+        own_out(1).wait_send()
+        own_out(3).start()
+
+    for copy in local[5:]:
         copy.wait()
     cache_out.wait_recv()
     positions = half_len // rows
@@ -322,11 +331,32 @@
 
     blocks = rows // SLOTS
     lax.fori_loop(0, 3, attend, 0)
-    relay(2, (2, 1))
+
+    @pl.when(is_mid)
+    def _():
+        relay(2, 2)
+        relay(1, 0)
+        rows_across(1).start()
+
+    @pl.when(is_end)
+    def _():
+        own_out(2).wait_send()
+        rows_beside.start()
+
     lax.fori_loop(3, 6, attend, 0)
-    relay(3, (2, 1))
+
+    @pl.when(is_mid)
+    def _():
+        relay(2, 3)
+        relay(1, 1)
+
+    @pl.when(is_end)
+    def _():
+        own_out(3).wait_send()
+        rows_diagonal.start()
+
+    rows_across(3).start()
     lax.fori_loop(6, blocks, attend, 0)
-    relay(4, (2, 1))
 
     def project(first, second, slot, cols, so_far):
         both = jnp.concatenate([first[:, cols], second[:, cols]], axis=0)
@@ -355,7 +385,18 @@
             shrink = project(grouped.at[2 * q], from_x.at[q], q, pl.ds(k * step, step), shrink)
         finish(q, q, shrink)
 
+    @pl.when(is_mid)
+    def _():
+        relay(1, 2)
+        relay(3, 0)
+        relay(1, 3)
+        relay(3, 1)
+
     relation_of(0)
+
+    @pl.when(is_mid)
+    def _():
+        relay(3, 2)
 
     @pl.when(is_end)
     def _():
@@ -366,10 +407,8 @@
 
     @pl.when(is_mid)
     def _():
+        relay(3, 3)
         relation_of(1)
-        for k in pieces:
-            arrived(3, k)
-            forward(3, k).start()
 
     result_beside = remote(to_end.at[0], deltas.at[2], dsend.at[4], drecv.at[2], beside)
     result_diagonal = remote(to_end.at[1], deltas.at[3], dsend.at[5], drecv.at[3], diagonal)
@@ -390,8 +429,8 @@
 
     @pl.when(is_end)
     def _():
-        arrived(3, 0)
-        relation_of(3, lambda k: arrived(3, k + 1))
+        arrived(3, CHUNKS)
+        relation_of(3, lambda k: arrived(3, k))
         result_beside.wait_recv()
         result_diagonal.wait_recv()
 
@@ -425,8 +464,7 @@
 
     value_out.wait_send()
     cache_out.wait_send()
-    for copy in own_out:
-        copy.wait_send()
+    own_out(CHUNKS).wait_send()
     for q in (0, 2, 3):
         rows_across(q).wait_send()
         delta_out(q).wait_send()
@@ -438,6 +476,8 @@
 
     @pl.when(is_mid)
     def _():
+        for k in range(CHUNKS):
+            own_out(k).wait_send()
         rows_across(1).wait_send()
         delta_out(1).wait_send()
         result_beside.wait_send()
@@ -466,15 +506,16 @@
     down = jnp.swapaxes(adapter_down_weight[0], 0, 1)
     cache = key_value_cache.reshape(rows * local_len, 2 * HEAD_SIZE)
     blocks, tall = rows // SLOTS, 2 * HQ * SLOTS
-    anywhere = pl.BlockSpec(memory_space=pl.ANY)
-    vmem = pl.BlockSpec(memory_space=pltpu.VMEM)
     dma = pltpu.SemaphoreType.DMA
     return pl.pallas_call(
         fused_kernel,
         out_shape=jax.ShapeDtypeStruct(query.shape, bf16),
-        in_specs=[anywhere] * 7 + [vmem, vmem, pl.BlockSpec(memory_space=pltpu.SMEM)],
-        out_specs=vmem,
+        in_specs=[pl.BlockSpec(memory_space=pltpu.HBM)] * 10,
+        out_specs=pl.BlockSpec(memory_space=pltpu.VMEM),
         scratch_shapes=[
+            pltpu.VMEM((1, rows), jnp.int32),
+            pltpu.VMEM((1, rows), jnp.int32),
+            pltpu.SMEM(adapter_storage_index.shape, jnp.int32),
             pltpu.VMEM(hidden.shape, bf16),
             pltpu.VMEM((width, HEAD_SIZE), bf16),
             pltpu.VMEM((4, rank, width), bf16),
@@ -497,7 +538,7 @@
             pltpu.VMEM((rows, 1), jnp.int32),
             pltpu.VMEM((rows, rows), bf16),
             pltpu.VMEM((2, rows, HEAD_SIZE), bf16),
-            dma((7,)),
+            dma((10,)),
             dma((4, CHUNKS + 1)),
             dma((4, CHUNKS + 1)),
             dma((2,)),
@@ -509,7 +550,7 @@
             dma((2,)),
         ],
         compiler_params=pltpu.CompilerParams(
-            collective_id=0, has_side_effects=True, vmem_limit_bytes=40 * 1024 * 1024
+            collective_id=0, has_side_effects=True, vmem_limit_bytes=56 * 1024 * 1024
         ),
         cost_estimate=pl.CostEstimate(
             flops=2 * 4 * rows * width * HEAD_SIZE, bytes_accessed=6 << 20, transcendentals=rows * 2560

time: 56.3 us -> 45.5 us (0.81)
  local copies, waits for them, and re-layouts: 10.2 us -> 3.59 us
  Pallas kernels: 45.6 us -> 41.7 us
    unnamed x19 -> x1, local copies, waits for them, and re-layouts: 9.21 us -> 1.87 us
    pallas_call x1, Pallas kernels: 45.6 us -> 41.7 us  [fused_body(): pl.pallas_call(fused_kernel, out_shape=jax.ShapeDtypeStruct(query.shape,...]
    reshape x1, local copies, waits for them, and re-layouts: 1.01 us -> 1.72 us  [fused_body(): cache = key_value_cache.reshape(rows * local_len, 2 * HEAD_SIZE)]
where the time goes in v2:
time: 45.5 us; the launch traced here: 45.3 us
  Pallas kernels  41.7 us (92%)
  local copies, waits for them, and re-layouts  3.59 us (8%)
    pallas_call x1, Pallas kernels, fused_body(): pl.pallas_call(fused_kernel, out_shape=jax.ShapeDtypeStruct(query.shape,...  41.7 us
    unnamed x1, local copies, waits for them, and re-layouts  1.87 us
    reshape x1, local copies, waits for them, and re-layouts, fused_body(): cache = key_value_cache.reshape(rows * local_len, 2 * HEAD_SIZE)  1.72 us

profile of v2, /device:TPU:1, one launch (start us, length us, event | category | flops | bytes accessed | tf_op | source)
XLA Modules:
  0.0 45.3 jit_solution(5678466825200948457)
XLA Ops:
  0.0 1.7 %reshape.9.cache = bf16[512,256]{1,0:T(8,128)(2,1)} reshape(bf16[128,4,256]{2,1,0:T(4,128)(2,1)} %param.14) | data formatting | bytes 524288 | tf_op jit(solution)/shard_map/reshape | solution.py:507
  1.7 41.7 %shard_map.100 = bf16[2,128,1024]{2,1,0:T(8,128)(2,1)} custom-call(bf16[2,128,4096]{2,1,0:T(8,128)(2,1)} %hid.1, bf16[4096,128]{1,0:T(8,128)(2,1)} %wv.1, bf16[64,4096]{1,0:T(8,128)(2,1)} %bitcast.6, bf16[64,128]{1,0:T(8,128)(2,1)} %bitcast.7, bf16[512,256]{1,0:T(8,128)(2,1)} %reshape.9.cache, bf16[2,128,1024]{2,1,0:T(8,128)(2,1)} %query.1, ...), custom_call_target="tpu_custom_call" | custom-call | flops 536870912 | bytes 6291456 | tf_op jit(solution)/shard_map/pallas_call | solution.py:510
  43.5 1.9 %copy.12 = bf16[2,128,1024]{2,1,0:T(8,128)(2,1)} copy(bf16[2,128,1024]{2,1,0:T(8,128)(2,1)} %shard_map.100) | data formatting | bytes 1048576

commit v3 on v2

--- a/solution.py
+++ b/solution.py
@@ -173,7 +173,7 @@
 
     width = hb.shape[2]
     step = width // CHUNKS
-    half_len = cache.shape[0]
+    positions = cache.shape[1]
 
     local = [
         pltpu.make_async_copy(adapter_in, adapter, lsem.at[7]),
@@ -264,9 +264,16 @@
         return remote(grouped.at[2 * q + 1], from_x.at[q], gsend.at[2 * q + 1], grecv.at[q], across)
 
     rows_beside = remote(grouped.at[2], from_end.at[0], gsend.at[2], rrecv.at[0], beside)
-    rows_diagonal = remote(grouped.at[3], from_end.at[1], gsend.at[3], rrecv.at[1], diagonal)
+    rows_onward = remote(from_x.at[1], from_end.at[1], gsend.at[4], rrecv.at[1], beside)
     rows_across(0).start()
-    rows_across(2).start()
+
+    @pl.when(is_end)
+    def _():
+        rows_across(1).start()
+
+    @pl.when(is_mid)
+    def _():
+        rows_across(2).start()
 
     @pl.when(is_mid)
     def _():
@@ -286,27 +293,31 @@
     def _():
         relay(2, 1)
         own_out(3).start()
+        rows_across(1).start()
 
     @pl.when(is_end)
     def _():
         own_out(1).wait_send()
         own_out(3).start()
+        rows_across(2).start()
 
     for copy in local[5:]:
         copy.wait()
     cache_out.wait_recv()
-    positions = half_len // rows
     cached = 2 * positions * SLOTS
     inverse = HEAD_SIZE ** (-0.5)
 
     def attend(b, carry):
         at = pl.ds(pl.multiple_of(b * SLOTS, SLOTS), SLOTS)
-        cat = pl.ds(pl.multiple_of(b * SLOTS * positions, SLOTS * positions), SLOTS * positions)
+        cached_rows = [
+            kb[i, at].astype(jnp.float32).reshape(SLOTS * positions, 2 * HEAD_SIZE).astype(jnp.bfloat16)
+            for i in range(2)
+        ]
         q = jnp.concatenate(
             [qb[s, at, h * HEAD_SIZE:(h + 1) * HEAD_SIZE] for s in range(2) for h in range(HQ)], axis=0
         )
         keys = jnp.concatenate(
-            [kb[0, cat, :HEAD_SIZE], kb[1, cat, :HEAD_SIZE], fb[0, at, :], fb[1, at, :]], axis=0
+            [cached_rows[0][:, :HEAD_SIZE], cached_rows[1][:, :HEAD_SIZE], fb[0, at, :], fb[1, at, :]], axis=0
         )
         scores = mm(q, keys, NT) * inverse
         i = lax.broadcasted_iota(jnp.int32, scores.shape, 0)
@@ -324,7 +335,7 @@
         weights = jnp.where(ok, jnp.exp(masked - peak), 0.0)
         inv[b] = 1.0 / jnp.sum(weights, axis=1, keepdims=True)
         rounded = weights.astype(jnp.bfloat16)
-        values = jnp.concatenate([kb[0, cat, HEAD_SIZE:], kb[1, cat, HEAD_SIZE:]], axis=0)
+        values = jnp.concatenate([cached_rows[0][:, HEAD_SIZE:], cached_rows[1][:, HEAD_SIZE:]], axis=0)
         ctx[b] = mm(rounded[:, :cached], values)
         wnew[b] = rounded[:, cached:]
         return carry
@@ -336,13 +347,13 @@
     def _():
         relay(2, 2)
         relay(1, 0)
-        rows_across(1).start()
 
     @pl.when(is_end)
     def _():
         own_out(2).wait_send()
         rows_beside.start()
 
+    rows_across(3).start()
     lax.fori_loop(3, 6, attend, 0)
 
     @pl.when(is_mid)
@@ -353,9 +364,9 @@
     @pl.when(is_end)
     def _():
         own_out(3).wait_send()
-        rows_diagonal.start()
-
-    rows_across(3).start()
+        rows_across(1).wait_recv()
+        rows_onward.start()
+
     lax.fori_loop(6, blocks, attend, 0)
 
     def project(first, second, slot, cols, so_far):
@@ -416,7 +427,7 @@
     @pl.when(is_mid)
     def _():
         rows_beside.wait_recv()
-        rows_diagonal.wait_recv()
+        rows_onward.wait_recv()
         shrink = None
         for k in range(CHUNKS):
             shrink = project(from_end.at[0], from_end.at[1], 0, pl.ds(k * step, step), shrink)
@@ -465,20 +476,20 @@
     value_out.wait_send()
     cache_out.wait_send()
     own_out(CHUNKS).wait_send()
+    for q in range(4):
+        rows_across(q).wait_send()
     for q in (0, 2, 3):
-        rows_across(q).wait_send()
         delta_out(q).wait_send()
 
     @pl.when(is_end)
     def _():
         rows_beside.wait_send()
-        rows_diagonal.wait_send()
+        rows_onward.wait_send()
 
     @pl.when(is_mid)
     def _():
         for k in range(CHUNKS):
             own_out(k).wait_send()
-        rows_across(1).wait_send()
         delta_out(1).wait_send()
         result_beside.wait_send()
         result_diagonal.wait_send()
@@ -502,9 +513,7 @@
     bf16, f32 = jnp.bfloat16, jnp.float32
     _, rows, width = hidden.shape
     rank = adapter_down_weight.shape[2]
-    local_len = key_value_cache.shape[1]
     down = jnp.swapaxes(adapter_down_weight[0], 0, 1)
-    cache = key_value_cache.reshape(rows * local_len, 2 * HEAD_SIZE)
     blocks, tall = rows // SLOTS, 2 * HQ * SLOTS
     dma = pltpu.SemaphoreType.DMA
     return pl.pallas_call(
@@ -521,7 +530,7 @@
             pltpu.VMEM((4, rank, width), bf16),
             pltpu.VMEM((4, rank, HEAD_SIZE), bf16),
             pltpu.VMEM(query.shape, bf16),
-            pltpu.VMEM((2,) + cache.shape, bf16),
+            pltpu.VMEM((2,) + key_value_cache.shape, bf16),
             pltpu.VMEM(fresh_token_keys.shape, bf16),
             pltpu.VMEM((8, 2 * SLOTS, width), bf16),
             pltpu.VMEM((4, 2 * SLOTS, width), bf16),
@@ -560,7 +569,7 @@
         value_projection_weight,
         down,
         adapter_up_weight[0],
-        cache,
+        key_value_cache,
         query,
         fresh_token_keys,
         adapter_per_row.reshape(1, rows),

time: 45.5 us -> 43.8 us (0.963)
  local copies, waits for them, and re-layouts: 3.59 us -> 1.87 us
    reshape x1 -> x0, local copies, waits for them, and re-layouts: 1.72 us -> none  [fused_body(): cache = key_value_cache.reshape(rows * local_len, 2 * HEAD_SIZE)]
where the time goes in v3:
time: 43.8 us; the launch traced here: 43.6 us
  Pallas kernels  41.7 us (95%)
  local copies, waits for them, and re-layouts  1.87 us (4%)
    pallas_call x1, Pallas kernels, fused_body(): pl.pallas_call(fused_kernel, out_shape=jax.ShapeDtypeStruct(query.shape,...  41.7 us
    unnamed x1, local copies, waits for them, and re-layouts  1.87 us

profile of v3, /device:TPU:1, one launch (start us, length us, event | category | flops | bytes accessed | tf_op | source)
XLA Modules:
  0.0 43.6 jit_solution(1607872880353645798)
XLA Ops:
  0.0 41.7 %shard_map.100 = bf16[2,128,1024]{2,1,0:T(8,128)(2,1)} custom-call(bf16[2,128,4096]{2,1,0:T(8,128)(2,1)} %hid.1, bf16[4096,128]{1,0:T(8,128)(2,1)} %wv.1, bf16[64,4096]{1,0:T(8,128)(2,1)} %bitcast.6, bf16[64,128]{1,0:T(8,128)(2,1)} %bitcast.7, bf16[128,4,256]{2,1,0:T(4,128)(2,1)} %cache.1, bf16[2,128,1024]{2,1,0:T(8,128)(2,1)} %query.1, ...), custom_call_target="tpu_custom_call" | custom-call | flops 536870912 | bytes 6291456 | tf_op jit(solution)/shard_map/pallas_call | solution.py:519
  41.8 1.9 %copy.12 = bf16[2,128,1024]{2,1,0:T(8,128)(2,1)} copy(bf16[2,128,1024]{2,1,0:T(8,128)(2,1)} %shard_map.100) | data formatting | bytes 1048576
